TPU v7x, 256 devices: a whole 4x4x8 slice. The times are simulated.
256 devices in a mesh: island: 32 (over z, x), fsdp: 8 (over y, core).
Axes of the slice: x: 4, y: 4, z: 8, core: 2. Of those that a mesh axis runs over, the one named last changes fastest.
Arguments:
- gradient: bfloat16 [32, 2560, 4096], P('island', 'fsdp'), may hold values from -300 to 300, as said below
- momentum: bfloat16 [32, 2560, 4096], P('island', 'fsdp'), may hold values from -300 to 300, as said below
- drift: float32 [32, 2560, 4096], P('island', 'fsdp'), may hold values from -6 to 6
- outer_weights: float32 [2560, 4096], P('fsdp', 'island'), may hold values from -6 to 6
- outer_momentum: float32 [2560, 4096], P('fsdp', 'island'), may hold values from -6 to 6
Outputs:
- new_weights: float32 [2560, 4096], P('fsdp', 'island')
- new_momentum: float32 [2560, 4096], P('fsdp', 'island')
Inputs may be any that keep to these rules, and one draw needn't show every extreme that they name: `gradient`: real values. `momentum`: real values.
All inputs are finite; a program needn't handle non-finite values.
Results may differ from a plain program's by a relative error of at most 0.00075.
Values may be sent and summed in bfloat16 or wider, within the bound.
A program may use at most 64 MiB of HBM per device.

v0:
```python
import math

import jax
import jax.numpy as jnp
from jax import lax
from jax.sharding import PartitionSpec as P

ROWS = 2560
BLK = 512
NS_STEPS = 2


EPS = 1e-07
COEF_A = 3.4445
COEF_B = -4.775
COEF_C = 2.0315
BETA = 0.95
OUTER_BETA = 0.9
OUTER_LR = 0.7


def newton_steps(current):
    for sweep in range(NS_STEPS):
        gram = lax.dot_general(
            current, current, (((0,), (0,)), ((), ())), preferred_element_type=jnp.float32
        ).astype(jnp.bfloat16)
        square = jnp.dot(gram, gram, preferred_element_type=jnp.float32)
        poly = (COEF_B * gram.astype(jnp.float32) + COEF_C * square).astype(jnp.bfloat16)
        current = (
            COEF_A * current.astype(jnp.float32)
            + jnp.dot(current, poly, preferred_element_type=jnp.float32)
        ).astype(jnp.bfloat16)
    return current


def on_device(gradient, momentum, drift, outer_weights, outer_momentum):
    step_scale = 0.2 * math.sqrt(max(ROWS, BLK))
    grad_f = gradient[0].astype(jnp.float32)
    nesterov_in = grad_f + BETA * (BETA * momentum[0].astype(jnp.float32) + grad_f)
    drift_local = drift[0]
    whole_block = lax.all_to_all(nesterov_in, "fsdp", split_axis=1, concat_axis=0, tiled=True)
    norm_value = jnp.sqrt(jnp.sum(whole_block * whole_block))
    start = (whole_block / (norm_value + EPS)).astype(jnp.bfloat16)
    orth = newton_steps(start)
    update = lax.all_to_all(orth, "fsdp", split_axis=0, concat_axis=1, tiled=True)
    total = lax.psum_scatter(
        drift_local + step_scale * update.astype(jnp.float32),
        "island",
        scatter_dimension=1,
        tiled=True,
    )
    pseudo = total / lax.axis_size("island")
    new_momentum = OUTER_BETA * outer_momentum + pseudo
    new_weights = outer_weights - OUTER_LR * (pseudo + OUTER_BETA * new_momentum)
    return (new_weights, new_momentum)


def solution(mesh):
    in_specs = (
        P("island", "fsdp", None),
        P("island", "fsdp", None),
        P("island", "fsdp", None),
        P("fsdp", "island"),
        P("fsdp", "island"),
    )
    out_specs = (P("fsdp", "island"), P("fsdp", "island"))
    return jax.shard_map(
        on_device, mesh=mesh, in_specs=in_specs, out_specs=out_specs, check_vma=False
    )
```

profile of v0, /device:TPU:1, one launch (start us, length us, event | category | flops | bytes accessed | tf_op | source)
XLA Modules:
  0.0 381.7 jit_solution(12995974255262916058)
XLA Ops:
  7.2 0.0 copy-start.1
  7.2 0.0 reduce-scatter.2.cloned.1.call-start
  7.2 3.1 copy.13
  10.3 0.0 copy-done.1
  10.3 0.6 convert_multiply_fusion
  11.0 4.9 %copy.14 = f32[40,8,8,512]{3,2,1,0:T(8,128)S(1)} copy(f32[40,8,8,512]{3,1,2,0:T(8,128)S(1)} %bitcast.35) | data formatting | bytes 10485760
  15.9 6.3 %fusion.1 = f32[320,8,512]{2,0,1:T(8,128)S(1)} fusion(f32[320,8,512]{2,1,0:T(8,128)S(1)} %bitcast.36, f32[320,8,512]{2,1,0:T(8,128)S(1)} %bitcast.38), kind=kLoop, calls=%fused_computation.3 | loop fusion | flops 3932160 | bytes 15728640 | tf_op jit(solution)/shard_map/add | solution.py:39
  22.1 66.5 %all_to_all.23 = f32[320,8,512]{2,0,1:T(8,128)S(1)} all-to-all(f32[320,8,512]{2,0,1:T(8,128)S(1)} %fusion.1), channel_id=1, replica_groups=mesh['island'=32,'fsdp'=8] {'fsdp'}, dimensions={1} | all-to-all | bytes 10485760 | tf_op jit(solution)/shard_map/all_to_all | solution.py:41
  88.6 0.0 copy-start
  88.6 2.3 copy-done
  90.9 1.9 multiply_reduce_fusion
  93.5 3.2 divide_convert_fusion
  96.8 1.5 fusion.11
  98.3 3.7 add_convert_fusion.1
  102.1 4.1 %convolution_convert_fusion = bf16[512,512]{1,0:T(8,128)(2,1)S(1)} fusion(bf16[2560,512]{1,0:T(8,128)(2,1)} %add_convert_fusion.1), kind=kOutput, calls=%fused_computation.20 | convolution fusion | flops 1342439424 | bytes 3145728 | tf_op jit(solution)/shard_map/dot_general | solution.py:24
  106.1 4.4 %add_convert_fusion = bf16[2560,512]{1,0:T(8,128)(2,1)S(1)} fusion(bf16[2560,512]{1,0:T(8,128)(2,1)} %add_convert_fusion.1, bf16[512,512]{1,0:T(8,128)(2,1)S(1)} %convolution_convert_fusion), kind=kOutput, calls=%fused_computation.5 | convolution fusion | flops 1617166336 | bytes 5767168 | tf_op jit(solution)/shard_map/dot_general | solution.py:31
  110.6 35.7 %all_to_all.24 = bf16[8,320,512]{2,1,0:T(8,128)(2,1)S(1)} all-to-all(bf16[8,320,512]{2,1,0:T(8,128)(2,1)S(1)} %bitcast.42), channel_id=1, replica_groups=mesh['island'=32,'fsdp'=8] {'fsdp'}, dimensions={0} | all-to-all | bytes 5242880 | tf_op jit(solution)/shard_map/all_to_all | solution.py:45
  146.2 0.0 slice-start
  146.2 0.8 multiply_bitcast_fusion
  147.0 0.0 slice-start.1
  147.0 0.6 copy.12
  147.7 0.7 slice-done
  148.4 0.5 slice-done.1
  148.9 3.0 bitcast_add_fusion
  151.9 0.0 copy-start.2
  151.9 0.0 copy-start.3
  151.9 0.0 reduce-scatter.2.cloned.1.call-update
  151.9 221.2 %reduce-scatter.2.cloned.1.call-done = f32[320,128]{1,0:T(8,128)} async-done(((f32[320,4096]{1,0:T(8,128)}), f32[320,128]{1,0:T(8,128)}) %reduce-scatter.2.cloned.1.call-update) | async-done | bytes 163856 | tf_op jit(solution)/shard_map/reduce_scatter | solution.py:46
  373.1 0.0 copy-done.2
  373.1 0.0 copy-done.3
  373.1 1.7 multiply_subtract_fusion
  (1 shorter events, 0.0 us)
Async XLA Ops:
  7.2 3.2 copy-start.1
  7.2 365.9 %reduce-scatter.2.cloned.1.call-start = ((), (), s32[]{:S(2)}) async-start(), calls=%async_computation.3 | async-start | bytes 5406720 | tf_op jit(solution)/shard_map/reduce_scatter | solution.py:46
  88.6 2.3 copy-start
  146.2 2.2 slice-start
  147.0 1.9 slice-start.1
  151.9 221.2 %copy-start.2 = (f32[320,128]{1,0:T(8,128)S(1)}, f32[320,128]{1,0:T(8,128)}, u32[]{:S(2)}) copy-start(f32[320,128]{1,0:T(8,128)} %param.8) | copy-start | bytes 491524
  151.9 221.2 %copy-start.3 = (f32[320,128]{1,0:T(8,128)S(1)}, f32[320,128]{1,0:T(8,128)}, u32[]{:S(2)}) copy-start(f32[320,128]{1,0:T(8,128)} %param.9) | copy-start | bytes 491524
Sparse Core Ops, SparseCore 0:
  152.0 221.0 reduce-scatter.1
where the time goes:
time: 386 us; the launch traced here: 382 us
  waiting for transfers between devices  221 us (57%)
  blocking collectives  102 us (26%)
  other arithmetic  17.5 us (5%)
  between operations  14.8 us (4%)
  matrix products  13.8 us (4%)
  local copies, waits for them, and re-layouts  12.2 us (3%)
    reduce_scatter x1, waiting for transfers between devices, on_device(): lax.psum_scatter(drift_local + step_scale * update.astype(jnp.float32), '...  221 us
    all_to_all x1, blocking collectives, on_device(): lax.all_to_all(nesterov_in, 'fsdp', split_axis=1, concat_axis=0, tiled=True)  66.5 us
    all_to_all x1, blocking collectives, on_device(): lax.all_to_all(orth, 'fsdp', split_axis=0, concat_axis=1, tiled=True)  35.7 us
    unnamed x14, local copies, waits for them, and re-layouts  11.5 us
    dot_general x2, matrix products, newton_steps(): jnp.dot(current, poly, preferred_element_type=jnp.float32)  8.17 us
  transfers between devices with their start and end apart: 1, of which 1 were waited for; matrix products, arithmetic and copies ran while one was open for 0% of the time, Pallas kernels for 0%

commit v1 on v0

v1 whole, which is shorter than its diff:
```python
import functools
import math

import jax
import jax.numpy as jnp
from jax import lax
from jax.experimental import pallas as pl
from jax.experimental.pallas import tpu as pltpu
from jax.sharding import PartitionSpec as P

ROWS = 2560
BLK = 512
EPS = 1e-07
COEF_A = 3.4445
COEF_B = -4.775
COEF_C = 2.0315
BETA = 0.95
OUTER_BETA = 0.9
OUTER_LR = 0.7
STEP_SCALE = 0.2 * math.sqrt(max(ROWS, BLK))

MESH = pl.DeviceIdType.MESH
F32 = jnp.float32
BF16 = jnp.bfloat16
NZ, NX, NY = 8, 4, 4
NF = 2 * NY
LANES = 128
GROUPS = ((4, 3), (5, 2), (6, 1), (7, 0))
SENDS = tuple((dy, core) for core in (0, 1) for dy in (2, 1, 3, 0))
CODE1, CODE2, CODE4 = 14.0, 7.0, 3.5
STEP_ROWS = 64


def code(v, c):
    return jnp.exp(v * c).astype(BF16)


def decode(y, c):
    return jnp.log(y.astype(F32)) * (1.0 / c)


def plain(v, c):
    return v.astype(BF16)


def unplain(y, c):
    return y.astype(F32)


def kernel(
    g_hbm, m_hbm, d_hbm, ow_ref, om_ref, nw_ref, nm_ref,
    gbuf, mbuf, dbuf, xs, xr, gram,
    de, dd2, dl1, dr1, dzs, dzr, dacc,
    oe, od2, ol1, or1, ozs, ozr, oacc, tsend, trecv,
    load_sem, ysend, yrecv,
    d2send, d2recv, d1send, d1recv, dzsend, dzrecv,
    o2send, o2recv, o1send, o1recv, ozsend, ozrecv, tsem,
):
    isl = lax.axis_index("island")
    f = lax.axis_index("fsdp")
    z, x = isl // NX, isl % NX
    y, core = f // 2, f % 2
    rows = g_hbm.shape[1]
    chunks = rows // STEP_ROWS
    right = (z * NX + (x + 1) % NX, f)
    left = (z * NX + (x + NX - 1) % NX, f)
    x_right, x_left, x_far = (x + 1) % NX, (x + NX - 1) % NX, (x + 2) % NX
    swap = (f * NX + x, z)

    def at_fsdp(dy, c):
        return ((y + dy) % NY) * 2 + c

    barrier = pltpu.get_barrier_semaphore()

    def greet(dev):
        pl.semaphore_signal(barrier, inc=1, device_id=dev, device_id_type=MESH)

    for d in range(1, NF):
        greet((isl, (f + d) % NF))
    for d in range(1, NZ):
        greet((((z + d) % NZ) * NX + x, f))
    greet(right)
    greet(left)

    @pl.when(z != f)
    def _():
        greet(swap)

    def g_load(j):
        cols = pl.ds(pl.multiple_of(at_fsdp(*SENDS[j]) * BLK, BLK), BLK)
        return (
            pltpu.make_async_copy(g_hbm.at[0, :, cols], gbuf.at[j], load_sem.at[j]),
            pltpu.make_async_copy(m_hbm.at[0, :, cols], mbuf.at[j], load_sem.at[NF + j]),
        )

    def d_load(k):
        cols = pl.ds(pl.multiple_of(((z + k) % NZ) * BLK, BLK), BLK)
        return pltpu.make_async_copy(d_hbm.at[0, :, cols], dbuf.at[k], load_sem.at[2 * NF + k])

    for j in range(NF):
        for copy in g_load(j):
            copy.start()
    for group in GROUPS:
        for k in group:
            d_load(k).start()

    pl.semaphore_wait(barrier, NF - 1 + NZ - 1 + 2 + jnp.where(z != f, 1, 0))

    def y_copy(j):
        dest = at_fsdp(*SENDS[j])
        return pltpu.make_async_remote_copy(
            src_ref=xs.at[j], dst_ref=xr.at[f], send_sem=ysend.at[j], recv_sem=yrecv.at[f],
            device_id=(isl, dest), device_id_type=MESH,
        )

    for j in range(NF):
        for copy in g_load(j):
            copy.wait()
        dy, c = SENDS[j]

        def nesterov(dst):
            @pl.loop(0, chunks)
            def _(i):
                r = pl.ds(pl.multiple_of(i * STEP_ROWS, STEP_ROWS), STEP_ROWS)
                grad = gbuf[j, r, :].astype(F32)
                mom = mbuf[j, r, :].astype(F32)
                dst[r, :] = (grad + BETA * (BETA * mom + grad)).astype(BF16)

        if dy:
            nesterov(xs.at[j])
            y_copy(j).start()
        else:
            @pl.when(core == c)
            def _():
                nesterov(xr.at[f])

            @pl.when(core != c)
            def _():
                nesterov(xs.at[j])
                y_copy(j).start()

    def reduction(enc, dec, c1, c2, c4, e, d2, l1, r1, zs, zr, acc, own, s2, v2, s1, v1, sz, vz):
        def rc(src, dst, ss, rs, dev):
            return pltpu.make_async_remote_copy(
                src_ref=src, dst_ref=dst, send_sem=ss, recv_sem=rs, device_id=dev, device_id_type=MESH
            )

        def far(k, to_right):
            return rc(e.at[k, x_far], d2.at[k], s2.at[k], v2.at[k], right if to_right else left)

        def near(k, to_right):
            if to_right:
                return rc(e.at[k, x_right], l1.at[k], s1.at[k], v1.at[k], right)
            return rc(e.at[k, x_left], r1.at[k], s1.at[NZ + k], v1.at[NZ + k], left)

        def zcopy(k):
            dev = (((z + k) % NZ) * NX + x, f)
            return rc(zs.at[k], zr.at[k], sz.at[k], vz.at[k], dev)

        def start(group):
            a, b = group
            far(a, True).start()
            far(b, False).start()
            near(b, True).start()
            near(a, False).start()

        def relay(group):
            for k, to_right in zip(group, (True, False)):
                far(k, to_right).wait_recv()
                mine = x_right if to_right else x_left
                e[k, mine] = enc(dec(e[k, mine], c1) + dec(d2[k], c1), c2)
                near(k, to_right).start()

        def total(group):
            for k, relayed_right in zip(group, (True, False)):
                near(k, True).wait_recv()
                near(k, False).wait_recv()
                cl, cr = (c2, c1) if relayed_right else (c1, c2)
                part = own(k) + dec(l1[k], cl) + dec(r1[k], cr)
                if k:
                    zs[k] = enc(part, c4)
                    zcopy(k).start()
                else:
                    acc[...] = part

        def finish():
            part = acc[...]
            for k in range(1, NZ):
                zcopy(k).wait_recv()
                part = part + dec(zr[k], c4)
            acc[...] = part

        def drain():
            for a, b in GROUPS:
                far(a, True).wait_send()
                far(b, False).wait_send()
            for k in range(NZ):
                near(k, True).wait_send()
                near(k, False).wait_send()
                if k:
                    zcopy(k).wait_send()

        return start, relay, total, finish, drain

    def piece(ref, k):
        return ref[k, :, pl.ds(pl.multiple_of(x * LANES, LANES), LANES)]

    d_start, d_relay, d_total, d_finish, d_drain = reduction(
        code, decode, CODE1, CODE2, CODE4, de, dd2, dl1, dr1, dzs, dzr, dacc,
        lambda k: piece(dbuf, k), d2send, d2recv, d1send, d1recv, dzsend, dzrecv,
    )
    o_start, o_relay, o_total, o_finish, o_drain = reduction(
        plain, unplain, 1, 1, 1, oe, od2, ol1, or1, ozs, ozr, oacc,
        lambda k: oe[k, x].astype(F32), o2send, o2recv, o1send, o1recv, ozsend, ozrecv,
    )

    def d_encode(group):
        for k in group:
            d_load(k).wait()

            @pl.loop(0, chunks)
            def _(i):
                r = pl.ds(pl.multiple_of(i * STEP_ROWS, STEP_ROWS), STEP_ROWS)
                for q in range(NX):
                    de[k, q, r, :] = code(dbuf[k, r, q * LANES:(q + 1) * LANES], CODE1)

    def schedule(prepare, start, relay, total):
        prepare(GROUPS[0])
        start(GROUPS[0])
        prepare(GROUPS[1])
        start(GROUPS[1])
        for s in range(4):
            if s + 2 < 4:
                prepare(GROUPS[s + 2])
                start(GROUPS[s + 2])
            relay(GROUPS[s])
            if s:
                total(GROUPS[s - 1])
        total(GROUPS[3])

    schedule(d_encode, d_start, d_relay, d_total)

    def y_arrival(source):
        return pltpu.make_async_remote_copy(
            src_ref=xs.at[0], dst_ref=xr.at[source], send_sem=ysend.at[0], recv_sem=yrecv.at[source],
            device_id=(isl, source), device_id_type=MESH,
        )

    contract_rows = (((0,), (0,)), ((), ()))
    for step, dy in enumerate((0, 1, 3, 2)):
        first = ((y + dy) % NY) * 2
        if dy:
            y_arrival(first).wait_recv()
            y_arrival(first + 1).wait_recv()
        else:
            y_arrival(first + 1 - core).wait_recv()
        part = xr[pl.ds(first, 2)].reshape(2 * rows, BLK)
        partial = lax.dot_general(part, part, contract_rows, preferred_element_type=F32)
        if step:
            gram[...] += partial
        else:
            gram[...] = partial

    raw = gram[...]
    row_id = lax.broadcasted_iota(jnp.int32, (BLK, BLK), 0)
    col_id = lax.broadcasted_iota(jnp.int32, (BLK, BLK), 1)
    square_norm = jnp.sum(jnp.where(row_id == col_id, raw, 0.0))
    norm = jnp.sqrt(jnp.full((1, 1), square_norm, F32))
    inverse = 1.0 / (norm + EPS)
    gram1 = (raw * inverse * inverse).astype(BF16)

    def dot(a, b):
        return jnp.dot(a, b, preferred_element_type=F32)

    poly1 = (COEF_B * gram1.astype(F32) + COEF_C * dot(gram1, gram1)).astype(BF16)
    half = (COEF_A * gram1.astype(F32) + dot(gram1, poly1)).astype(BF16)
    gram2 = (COEF_A * half.astype(F32) + dot(poly1, half)).astype(BF16)
    poly2 = (COEF_B * gram2.astype(F32) + COEF_C * dot(gram2, gram2)).astype(BF16)
    both = (
        COEF_A * (poly1.astype(F32) + poly2.astype(F32)) + dot(poly1, poly2)
    ).astype(BF16)

    def orth(group):
        for k in group:
            block = xr[(z + k) % NZ]
            out = (COEF_A * COEF_A) * block.astype(F32) + dot(block, both)
            out = (out * inverse).astype(BF16)
            for q in range(NX):
                oe[k, q] = out[:, q * LANES:(q + 1) * LANES]

    schedule(orth, o_start, o_relay, o_total)
    d_finish()
    o_finish()

    swap_copy = pltpu.make_async_remote_copy(
        src_ref=tsend, dst_ref=trecv, send_sem=tsem.at[0], recv_sem=tsem.at[1],
        device_id=swap, device_id_type=MESH,
    )
    tsend[...] = oacc[...].astype(BF16)

    @pl.when(z != f)
    def _():
        swap_copy.start()
        swap_copy.wait_recv()
        oacc[...] = trecv[...].astype(F32)

    pseudo = (dacc[...] + STEP_SCALE * oacc[...]) * (1.0 / (NZ * NX))
    momentum = OUTER_BETA * om_ref[...] + pseudo
    nm_ref[...] = momentum
    nw_ref[...] = ow_ref[...] - OUTER_LR * (pseudo + OUTER_BETA * momentum)

    for j in range(NF):
        dy, c = SENDS[j]
        if dy:
            y_copy(j).wait_send()
        else:
            @pl.when(core != c)
            def _():
                y_copy(j).wait_send()
    d_drain()
    o_drain()

    @pl.when(z != f)
    def _():
        swap_copy.wait_send()


def on_device(gradient, momentum, drift, outer_weights, outer_momentum):
    rows = gradient.shape[1]
    vmem = pl.BlockSpec(memory_space=pltpu.VMEM)
    hbm = pl.BlockSpec(memory_space=pl.ANY)
    out = jax.ShapeDtypeStruct((rows, LANES), F32)

    def reduce_buffers():
        piece = (rows, LANES)
        return [
            pltpu.VMEM((NZ, NX) + piece, BF16),
            pltpu.VMEM((NZ,) + piece, BF16),
            pltpu.VMEM((NZ,) + piece, BF16),
            pltpu.VMEM((NZ,) + piece, BF16),
            pltpu.VMEM((NZ,) + piece, BF16),
            pltpu.VMEM((NZ,) + piece, BF16),
            pltpu.VMEM(piece, F32),
        ]

    def sems(n):
        return pltpu.SemaphoreType.DMA((n,))

    reduce_sems = [sems(NZ), sems(NZ), sems(2 * NZ), sems(2 * NZ), sems(NZ), sems(NZ)]
    call = pl.pallas_call(
        kernel,
        out_shape=(out, out),
        in_specs=[hbm, hbm, hbm, vmem, vmem],
        out_specs=(vmem, vmem),
        scratch_shapes=[
            pltpu.VMEM((NF, rows, BLK), BF16),
            pltpu.VMEM((NF, rows, BLK), BF16),
            pltpu.VMEM((NZ, rows, BLK), F32),
            pltpu.VMEM((NF, rows, BLK), BF16),
            pltpu.VMEM((NF, rows, BLK), BF16),
            pltpu.VMEM((BLK, BLK), F32),
            *reduce_buffers(),
            *reduce_buffers(),
            pltpu.VMEM((rows, LANES), BF16),
            pltpu.VMEM((rows, LANES), BF16),
            sems(3 * NF),
            sems(NF),
            sems(NF),
            *reduce_sems,
            *reduce_sems,
            sems(2),
        ],
        compiler_params=pltpu.CompilerParams(
            collective_id=0, has_side_effects=True, vmem_limit_bytes=56 * 2**20
        ),
        name="outer_step",
    )
    return call(gradient, momentum, drift, outer_weights, outer_momentum)


def solution(mesh):
    in_specs = (
        P("island", "fsdp", None),
        P("island", "fsdp", None),
        P("island", "fsdp", None),
        P("fsdp", "island"),
        P("fsdp", "island"),
    )
    out_specs = (P("fsdp", "island"), P("fsdp", "island"))
    return jax.shard_map(
        on_device, mesh=mesh, in_specs=in_specs, out_specs=out_specs, check_vma=False
    )
```

time: 386 us -> 86.2 us (0.22)
  the two profiles are of different devices: /device:TPU:1 before, /device:TPU:9 now
where the time goes in v1:
time: 86.2 us; the launch traced here: 86.1 us
  Pallas kernels  82.3 us (95%)
  local copies, waits for them, and re-layouts  3.18 us (4%)
    pallas_call x1, Pallas kernels, on_device(): return call(gradient, momentum, drift, outer_weights, outer_momentum)  82.3 us
    unnamed x2, local copies, waits for them, and re-layouts  3.18 us

profile of v1, /device:TPU:9, one launch (start us, length us, event | category | flops | bytes accessed | tf_op | source)
XLA Modules:
  0.0 86.1 jit_solution(17573509131256830085)
XLA Ops:
  0.6 82.3 %outer_step.1 = (f32[320,128]{1,0:T(8,128)}, f32[320,128]{1,0:T(8,128)}) custom-call(bf16[1,320,4096]{2,1,0:T(8,128)(2,1)} %g_hbm.1, bf16[1,320,4096]{2,1,0:T(8,128)(2,1)} %m_hbm.1, f32[1,320,4096]{2,1,0:T(8,128)} %d_hbm.1, f32[320,128]{1,0:T(8,128)} %ow_ref.1, f32[320,128]{1,0:T(8,128)} %om_ref.1), custom_call_target="tpu_custom_call" | custom-call | tf_op jit(solution)/shard_map/outer_step/pallas_call | solution.py:378
  82.9 1.6 %copy.9 = f32[320,128]{1,0:T(8,128)} copy(f32[320,128]{1,0:T(8,128)} %get-tuple-element.4) | data formatting | bytes 327680
  84.5 1.6 %copy.10 = f32[320,128]{1,0:T(8,128)} copy(f32[320,128]{1,0:T(8,128)} %get-tuple-element.5) | data formatting | bytes 327680

commit v2 on v1

v2 whole, which is shorter than its diff:
```python
import functools
import math

import jax
import jax.numpy as jnp
from jax import lax
from jax.experimental import pallas as pl
from jax.experimental.pallas import tpu as pltpu
from jax.sharding import PartitionSpec as P

ROWS = 2560
BLK = 512
EPS = 1e-07
COEF_A = 3.4445
COEF_B = -4.775
COEF_C = 2.0315
BETA = 0.95
OUTER_BETA = 0.9
OUTER_LR = 0.7
STEP_SCALE = 0.2 * math.sqrt(max(ROWS, BLK))

MESH = pl.DeviceIdType.MESH
F32 = jnp.float32
BF16 = jnp.bfloat16
NZ, NX, NY = 8, 4, 4
NF = 2 * NY
LANES = 128
GROUPS = ((4, 3), (5, 2), (6, 1), (7, 0))
SENDS = tuple((dy, core) for core in (0, 1) for dy in (2, 1, 3, 0))
CODE = 3.6
STEP_ROWS = 64


def kernel(
    g_hbm, m_hbm, d_hbm, out_ref,
    gbuf, mbuf, dbuf, xs, xr, gram, both, scale,
    de, dd2, dl1, dr1, dzs, dzr, dacc,
    oe, od2, ol1, or1, ozs, ozr, oacc, tsend, trecv,
    load_sem, ysend, yrecv,
    d2send, d2recv, d1send, d1recv, dzsend, dzrecv,
    o2send, o2recv, o1send, o1recv, ozsend, ozrecv, tsem,
):
    isl = lax.axis_index("island")
    f = lax.axis_index("fsdp")
    z, x = isl // NX, isl % NX
    y, core = f // 2, f % 2
    rows = g_hbm.shape[1]
    chunks = rows // STEP_ROWS
    right = (z * NX + (x + 1) % NX, f)
    left = (z * NX + (x + NX - 1) % NX, f)
    x_right, x_left, x_far = (x + 1) % NX, (x + NX - 1) % NX, (x + 2) % NX
    swap = (f * NX + x, z)

    def at_fsdp(dy, c):
        return ((y + dy) % NY) * 2 + c

    barrier = pltpu.get_barrier_semaphore()

    def greet(dev):
        pl.semaphore_signal(barrier, inc=1, device_id=dev, device_id_type=MESH)

    for d in range(1, NF):
        greet((isl, (f + d) % NF))
    for d in range(1, NZ):
        greet((((z + d) % NZ) * NX + x, f))
    greet(right)
    greet(left)

    @pl.when(z != f)
    def _():
        greet(swap)

    def g_load(j):
        cols = pl.ds(pl.multiple_of(at_fsdp(*SENDS[j]) * BLK, BLK), BLK)
        return (
            pltpu.make_async_copy(g_hbm.at[0, :, cols], gbuf.at[j], load_sem.at[j]),
            pltpu.make_async_copy(m_hbm.at[0, :, cols], mbuf.at[j], load_sem.at[NF + j]),
        )

    def d_load(k):
        cols = pl.ds(pl.multiple_of(((z + k) % NZ) * BLK, BLK), BLK)
        return pltpu.make_async_copy(d_hbm.at[0, :, cols], dbuf.at[k], load_sem.at[2 * NF + k])

    for j in range(NF):
        for copy in g_load(j):
            copy.start()

    def y_copy(j):
        dest = at_fsdp(*SENDS[j])
        return pltpu.make_async_remote_copy(
            src_ref=xs.at[j], dst_ref=xr.at[f], send_sem=ysend.at[j], recv_sem=yrecv.at[f],
            device_id=(isl, dest), device_id_type=MESH,
        )

    for j in range(NF):
        for copy in g_load(j):
            copy.wait()
        if j == NY - 1:
            for group in GROUPS:
                for k in group:
                    d_load(k).start()
        dy, c = SENDS[j]

        def nesterov(dst):
            @pl.loop(0, chunks)
            def _(i):
                r = pl.ds(pl.multiple_of(i * STEP_ROWS, STEP_ROWS), STEP_ROWS)
                grad = gbuf[j, r, :].astype(F32)
                mom = mbuf[j, r, :].astype(F32)
                dst[r, :] = (grad + BETA * (BETA * mom + grad)).astype(BF16)

        if dy:
            nesterov(xs.at[j])
            if j == 0:
                pl.semaphore_wait(barrier, NF - 1 + NZ - 1 + 2 + jnp.where(z != f, 1, 0))
            if j < NY:
                y_copy(j).start()
        else:
            @pl.when(core == c)
            def _():
                nesterov(xr.at[f])

            @pl.when(core != c)
            def _():
                nesterov(xs.at[j])
                y_copy(j).start()

    def reduction(merge, finish_with, e, d2, l1, r1, zs, zr, acc, own, s2, v2, s1, v1, sz, vz):
        def rc(src, dst, ss, rs, dev):
            return pltpu.make_async_remote_copy(
                src_ref=src, dst_ref=dst, send_sem=ss, recv_sem=rs, device_id=dev, device_id_type=MESH
            )

        def far(k, to_right):
            return rc(e.at[k, x_far], d2.at[k], s2.at[k], v2.at[k], right if to_right else left)

        def near(k, to_right):
            if to_right:
                return rc(e.at[k, x_right], l1.at[k], s1.at[k], v1.at[k], right)
            return rc(e.at[k, x_left], r1.at[k], s1.at[NZ + k], v1.at[NZ + k], left)

        def zcopy(k):
            dev = (((z + k) % NZ) * NX + x, f)
            return rc(zs.at[k], zr.at[k], sz.at[k], vz.at[k], dev)

        def start_far(group):
            far(group[0], True).start()
            far(group[1], False).start()

        def start_near(group):
            near(group[1], True).start()
            near(group[0], False).start()

        def relay(group):
            for k, to_right in zip(group, (True, False)):
                far(k, to_right).wait_recv()
                mine = x_right if to_right else x_left
                e[k, mine] = merge(own(k, mine), d2[k].astype(F32)).astype(BF16)
                near(k, to_right).start()

        def total(group):
            for k in group:
                near(k, True).wait_recv()
                near(k, False).wait_recv()
                part = merge(merge(own(k, x), l1[k].astype(F32)), r1[k].astype(F32))
                if k:
                    zs[k] = part.astype(BF16)
                    zcopy(k).start()
                else:
                    acc[...] = finish_with(part)

        def finish():
            part = acc[...]
            for k in range(1, NZ):
                zcopy(k).wait_recv()
                part = part + finish_with(zr[k].astype(F32))
            acc[...] = part

        def drain():
            for a, b in GROUPS:
                far(a, True).wait_send()
                far(b, False).wait_send()
            for k in range(NZ):
                near(k, True).wait_send()
                near(k, False).wait_send()
                if k:
                    zcopy(k).wait_send()

        def run(prepare, between):
            prepare(GROUPS[0])
            start_far(GROUPS[0])
            start_near(GROUPS[0])
            prepare(GROUPS[1])
            start_far(GROUPS[1])
            for s in range(len(GROUPS)):
                if s + 2 < len(GROUPS):
                    prepare(GROUPS[s + 2])
                relay(GROUPS[s])
                if s + 1 < len(GROUPS):
                    start_near(GROUPS[s + 1])
                if s + 2 < len(GROUPS):
                    start_far(GROUPS[s + 2])
                if s:
                    total(GROUPS[s - 1])
                between(s)
            total(GROUPS[-1])

        return run, finish, drain

    def drift_code(k, q):
        return jnp.exp(CODE * dbuf[k, :, pl.ds(pl.multiple_of(q * LANES, LANES), LANES)])

    d_run, d_finish, d_drain = reduction(
        lambda a, b: a * b, lambda v: jnp.log(v) * (1.0 / CODE),
        de, dd2, dl1, dr1, dzs, dzr, dacc, drift_code,
        d2send, d2recv, d1send, d1recv, dzsend, dzrecv,
    )
    o_run, o_finish, o_drain = reduction(
        lambda a, b: a + b, lambda v: v,
        oe, od2, ol1, or1, ozs, ozr, oacc, lambda k, q: oe[k, q].astype(F32),
        o2send, o2recv, o1send, o1recv, ozsend, ozrecv,
    )

    def d_encode(group):
        far_first, far_second = group
        for k, near_side in ((far_first, x_left), (far_second, x_right)):
            d_load(k).wait()
            de[k, x_far] = drift_code(k, x_far).astype(BF16)
            de[k, near_side] = drift_code(k, near_side).astype(BF16)

    def y_arrival(source):
        return pltpu.make_async_remote_copy(
            src_ref=xs.at[0], dst_ref=xr.at[source], send_sem=ysend.at[0], recv_sem=yrecv.at[source],
            device_id=(isl, source), device_id_type=MESH,
        )

    contract_rows = (((0,), (0,)), ((), ()))

    def dot(a, b):
        return jnp.dot(a, b, preferred_element_type=F32)

    def newton():
        for step, dy in enumerate((0, 1, 3, 2)):
            first = ((y + dy) % NY) * 2
            if dy:
                y_arrival(first).wait_recv()
                y_arrival(first + 1).wait_recv()
            else:
                y_arrival(first + 1 - core).wait_recv()
            part = xr[pl.ds(first, 2)].reshape(2 * rows, BLK)
            partial = lax.dot_general(part, part, contract_rows, preferred_element_type=F32)
            if step:
                gram[...] += partial
            else:
                gram[...] = partial
        raw = gram[...]
        row_id = lax.broadcasted_iota(jnp.int32, (BLK, BLK), 0)
        col_id = lax.broadcasted_iota(jnp.int32, (BLK, BLK), 1)
        square_norm = jnp.sum(jnp.where(row_id == col_id, raw, 0.0))
        norm = jnp.sqrt(jnp.full((1, 1), square_norm, F32))
        inverse = 1.0 / (norm + EPS)
        gram1 = (raw * inverse * inverse).astype(BF16)
        poly1 = (COEF_B * gram1.astype(F32) + COEF_C * dot(gram1, gram1)).astype(BF16)
        half = (COEF_A * gram1.astype(F32) + dot(gram1, poly1)).astype(BF16)
        gram2 = (COEF_A * half.astype(F32) + dot(poly1, half)).astype(BF16)
        poly2 = (COEF_B * gram2.astype(F32) + COEF_C * dot(gram2, gram2)).astype(BF16)
        both[...] = (
            COEF_A * (poly1.astype(F32) + poly2.astype(F32)) + dot(poly1, poly2)
        ).astype(BF16)
        scale[...] = jnp.broadcast_to(inverse, scale.shape)

    def between(s):
        if s == 2:
            for j in range(NY):
                if SENDS[j][0]:
                    y_copy(j).wait_send()
            for j in range(NY, NF):
                if SENDS[j][0]:
                    y_copy(j).start()

            @pl.when(core == 0)
            def _():
                newton()

    d_run(d_encode, between)

    @pl.when(core == 1)
    def _():
        d_finish()
        newton()

    def orth(group):
        for k in group:
            block = xr[(z + k) % NZ]
            out = (COEF_A * COEF_A) * block.astype(F32) + dot(block, both[...])
            out = (out * scale[0:1, 0:1]).astype(BF16)
            for q in range(NX):
                oe[k, q] = out[:, q * LANES:(q + 1) * LANES]

    o_run(orth, lambda s: None)

    @pl.when(core == 0)
    def _():
        d_finish()

    o_finish()

    swap_copy = pltpu.make_async_remote_copy(
        src_ref=tsend, dst_ref=trecv, send_sem=tsem.at[0], recv_sem=tsem.at[1],
        device_id=swap, device_id_type=MESH,
    )
    tsend[...] = oacc[...].astype(BF16)

    @pl.when(z != f)
    def _():
        swap_copy.start()
        swap_copy.wait_recv()
        oacc[...] = trecv[...].astype(F32)

    out_ref[...] = dacc[...] + STEP_SCALE * oacc[...]

    for j in range(NF):
        dy, c = SENDS[j]
        if dy and j >= NY:
            y_copy(j).wait_send()
        if not dy:
            @pl.when(core != c)
            def _():
                y_copy(j).wait_send()
    d_drain()
    o_drain()

    @pl.when(z != f)
    def _():
        swap_copy.wait_send()


def on_device(gradient, momentum, drift, outer_weights, outer_momentum):
    rows = gradient.shape[1]
    vmem = pl.BlockSpec(memory_space=pltpu.VMEM)
    hbm = pl.BlockSpec(memory_space=pl.ANY)
    out = jax.ShapeDtypeStruct((rows, LANES), F32)

    def reduce_buffers():
        piece = (rows, LANES)
        return [
            pltpu.VMEM((NZ, NX) + piece, BF16),
            pltpu.VMEM((NZ,) + piece, BF16),
            pltpu.VMEM((NZ,) + piece, BF16),
            pltpu.VMEM((NZ,) + piece, BF16),
            pltpu.VMEM((NZ,) + piece, BF16),
            pltpu.VMEM((NZ,) + piece, BF16),
            pltpu.VMEM(piece, F32),
        ]

    def sems(n):
        return pltpu.SemaphoreType.DMA((n,))

    reduce_sems = [sems(NZ), sems(NZ), sems(2 * NZ), sems(2 * NZ), sems(NZ), sems(NZ)]
    call = pl.pallas_call(
        kernel,
        out_shape=out,
        in_specs=[hbm, hbm, hbm],
        out_specs=vmem,
        scratch_shapes=[
            pltpu.VMEM((NF, rows, BLK), BF16),
            pltpu.VMEM((NF, rows, BLK), BF16),
            pltpu.VMEM((NZ, rows, BLK), F32),
            pltpu.VMEM((NF, rows, BLK), BF16),
            pltpu.VMEM((NF, rows, BLK), BF16),
            pltpu.VMEM((BLK, BLK), F32),
            pltpu.VMEM((BLK, BLK), BF16),
            pltpu.VMEM((8, LANES), F32),
            *reduce_buffers(),
            *reduce_buffers(),
            pltpu.VMEM((rows, LANES), BF16),
            pltpu.VMEM((rows, LANES), BF16),
            sems(3 * NF),
            sems(NF),
            sems(NF),
            *reduce_sems,
            *reduce_sems,
            sems(2),
        ],
        compiler_params=pltpu.CompilerParams(
            collective_id=0, has_side_effects=True, vmem_limit_bytes=56 * 2**20
        ),
        name="outer_step",
    )
    total = call(gradient, momentum, drift)
    pseudo = total / (NZ * NX)
    new_momentum = OUTER_BETA * outer_momentum + pseudo
    new_weights = outer_weights - OUTER_LR * (pseudo + OUTER_BETA * new_momentum)
    return (new_weights, new_momentum)


def solution(mesh):
    in_specs = (
        P("island", "fsdp", None),
        P("island", "fsdp", None),
        P("island", "fsdp", None),
        P("fsdp", "island"),
        P("fsdp", "island"),
    )
    out_specs = (P("fsdp", "island"), P("fsdp", "island"))
    return jax.shard_map(
        on_device, mesh=mesh, in_specs=in_specs, out_specs=out_specs, check_vma=False
    )
```

time: 86.2 us -> 73.3 us (0.85)
  the two profiles are of different devices: /device:TPU:9 before, /device:TPU:1 now
where the time goes in v2:
time: 73.3 us; the launch traced here: 73.2 us
  Pallas kernels  70.9 us (97%)
  other arithmetic  1.68 us (2%)
    pallas_call x1, Pallas kernels, on_device(): total = call(gradient, momentum, drift)  70.9 us
    sub x1, other arithmetic, on_device(): outer_weights - OUTER_LR * (pseudo + OUTER_BETA * new_momentum)  1.68 us

profile of v2, /device:TPU:1, one launch (start us, length us, event | category | flops | bytes accessed | tf_op | source)
XLA Modules:
  0.0 73.2 jit_solution(1568444196483711438)
XLA Ops:
  0.6 0.0 copy-start.1
  0.6 0.0 copy-start
  0.7 70.9 %outer_step.1 = f32[320,128]{1,0:T(8,128)} custom-call(bf16[1,320,4096]{2,1,0:T(8,128)(2,1)} %g_hbm.1, bf16[1,320,4096]{2,1,0:T(8,128)(2,1)} %m_hbm.1, f32[1,320,4096]{2,1,0:T(8,128)} %d_hbm.1), custom_call_target="tpu_custom_call" | custom-call | tf_op jit(solution)/shard_map/outer_step/pallas_call | solution.py:390
  71.5 0.0 copy-done.1
  71.5 0.0 copy-done
  71.5 1.7 %multiply_subtract_fusion = (f32[320,128]{1,0:T(8,128)}, f32[320,128]{1,0:T(8,128)}) fusion(f32[320,128]{1,0:T(8,128)S(1)} %copy-done, f32[320,128]{1,0:T(8,128)} %outer_step.1, f32[320,128]{1,0:T(8,128)S(1)} %copy-done.1), kind=kLoop, calls=%fused_computation | loop fusion | flops 286720 | bytes 819200 | tf_op jit(solution)/shard_map/sub | solution.py:393
Async XLA Ops:
  0.6 70.9 %copy-start.1 = (f32[320,128]{1,0:T(8,128)S(1)}, f32[320,128]{1,0:T(8,128)}, u32[]{:S(2)}) copy-start(f32[320,128]{1,0:T(8,128)} %param.9) | copy-start | bytes 491524
  0.6 70.9 %copy-start = (f32[320,128]{1,0:T(8,128)S(1)}, f32[320,128]{1,0:T(8,128)}, u32[]{:S(2)}) copy-start(f32[320,128]{1,0:T(8,128)} %param.8) | copy-start | bytes 491524

commit v3 on v2

--- a/solution.py
+++ b/solution.py
@@ -25,20 +25,23 @@
 NZ, NX, NY = 8, 4, 4
 NF = 2 * NY
 LANES = 128
-GROUPS = ((4, 3), (5, 2), (6, 1), (7, 0))
+D_PAIRS = ((4, 3), (5, 2), (6, 1), (7, 0))
+O_PAIRS = ((4, 3), (5, 2), (6, 0))
+FOLDED = (1, 7)
 SENDS = tuple((dy, core) for core in (0, 1) for dy in (2, 1, 3, 0))
 CODE = 3.6
 STEP_ROWS = 64
+EARLY = 2
 
 
 def kernel(
     g_hbm, m_hbm, d_hbm, out_ref,
     gbuf, mbuf, dbuf, xs, xr, gram, both, scale,
     de, dd2, dl1, dr1, dzs, dzr, dacc,
-    oe, od2, ol1, or1, ozs, ozr, oacc, tsend, trecv,
+    oe, od2, ol1, or1, ozs, ozr, oacc, fold, tsend, trecv,
     load_sem, ysend, yrecv,
     d2send, d2recv, d1send, d1recv, dzsend, dzrecv,
-    o2send, o2recv, o1send, o1recv, ozsend, ozrecv, tsem,
+    o2send, o2recv, o1send, o1recv, ozsend, ozrecv, fold_sem, tsem,
 ):
     isl = lax.axis_index("island")
     f = lax.axis_index("fsdp")
@@ -81,9 +84,15 @@
         cols = pl.ds(pl.multiple_of(((z + k) % NZ) * BLK, BLK), BLK)
         return pltpu.make_async_copy(d_hbm.at[0, :, cols], dbuf.at[k], load_sem.at[2 * NF + k])
 
+    first_sends = NY - 1
     for j in range(NF):
         for copy in g_load(j):
             copy.start()
+        if j == first_sends - 1:
+            for k in D_PAIRS[0] + D_PAIRS[1]:
+                d_load(k).start()
+    for k in D_PAIRS[2] + D_PAIRS[3]:
+        d_load(k).start()
 
     def y_copy(j):
         dest = at_fsdp(*SENDS[j])
@@ -92,13 +101,9 @@
             device_id=(isl, dest), device_id_type=MESH,
         )
 
-    for j in range(NF):
+    def y_block(j):
         for copy in g_load(j):
             copy.wait()
-        if j == NY - 1:
-            for group in GROUPS:
-                for k in group:
-                    d_load(k).start()
         dy, c = SENDS[j]
 
         def nesterov(dst):
@@ -113,8 +118,7 @@
             nesterov(xs.at[j])
             if j == 0:
                 pl.semaphore_wait(barrier, NF - 1 + NZ - 1 + 2 + jnp.where(z != f, 1, 0))
-            if j < NY:
-                y_copy(j).start()
+            y_copy(j).start()
         else:
             @pl.when(core == c)
             def _():
@@ -125,7 +129,7 @@
                 nesterov(xs.at[j])
                 y_copy(j).start()
 
-    def reduction(merge, finish_with, e, d2, l1, r1, zs, zr, acc, own, s2, v2, s1, v1, sz, vz):
+    def reduction(groups, merge, finish_with, e, d2, l1, r1, zs, zr, acc, own, s2, v2, s1, v1, sz, vz):
         def rc(src, dst, ss, rs, dev):
             return pltpu.make_async_remote_copy(
                 src_ref=src, dst_ref=dst, send_sem=ss, recv_sem=rs, device_id=dev, device_id_type=MESH
@@ -143,23 +147,27 @@
             dev = (((z + k) % NZ) * NX + x, f)
             return rc(zs.at[k], zr.at[k], sz.at[k], vz.at[k], dev)
 
-        def start_far(group):
-            far(group[0], True).start()
-            far(group[1], False).start()
-
-        def start_near(group):
-            near(group[1], True).start()
-            near(group[0], False).start()
-
-        def relay(group):
-            for k, to_right in zip(group, (True, False)):
-                far(k, to_right).wait_recv()
-                mine = x_right if to_right else x_left
+        over_z = [k for group in groups for k in group if k]
+
+        goes_right = {k: n == 0 for group in groups for n, k in enumerate(group)}
+
+        def start_far(ks):
+            for k in ks:
+                far(k, goes_right[k]).start()
+
+        def start_near(ks):
+            for k in ks:
+                near(k, not goes_right[k]).start()
+
+        def relay(ks):
+            for k in ks:
+                far(k, goes_right[k]).wait_recv()
+                mine = x_right if goes_right[k] else x_left
                 e[k, mine] = merge(own(k, mine), d2[k].astype(F32)).astype(BF16)
-                near(k, to_right).start()
-
-        def total(group):
-            for k in group:
+                near(k, goes_right[k]).start()
+
+        def total(ks):
+            for k in ks:
                 near(k, True).wait_recv()
                 near(k, False).wait_recv()
                 part = merge(merge(own(k, x), l1[k].astype(F32)), r1[k].astype(F32))
@@ -171,52 +179,33 @@
 
         def finish():
             part = acc[...]
-            for k in range(1, NZ):
+            for k in over_z:
                 zcopy(k).wait_recv()
                 part = part + finish_with(zr[k].astype(F32))
             acc[...] = part
 
         def drain():
-            for a, b in GROUPS:
+            for a, b in groups:
                 far(a, True).wait_send()
                 far(b, False).wait_send()
-            for k in range(NZ):
-                near(k, True).wait_send()
-                near(k, False).wait_send()
-                if k:
-                    zcopy(k).wait_send()
-
-        def run(prepare, between):
-            prepare(GROUPS[0])
-            start_far(GROUPS[0])
-            start_near(GROUPS[0])
-            prepare(GROUPS[1])
-            start_far(GROUPS[1])
-            for s in range(len(GROUPS)):
-                if s + 2 < len(GROUPS):
-                    prepare(GROUPS[s + 2])
-                relay(GROUPS[s])
-                if s + 1 < len(GROUPS):
-                    start_near(GROUPS[s + 1])
-                if s + 2 < len(GROUPS):
-                    start_far(GROUPS[s + 2])
-                if s:
-                    total(GROUPS[s - 1])
-                between(s)
-            total(GROUPS[-1])
-
-        return run, finish, drain
+                for k in (a, b):
+                    near(k, True).wait_send()
+                    near(k, False).wait_send()
+            for k in over_z:
+                zcopy(k).wait_send()
+
+        return start_far, start_near, relay, total, finish, drain
 
     def drift_code(k, q):
         return jnp.exp(CODE * dbuf[k, :, pl.ds(pl.multiple_of(q * LANES, LANES), LANES)])
 
-    d_run, d_finish, d_drain = reduction(
-        lambda a, b: a * b, lambda v: jnp.log(v) * (1.0 / CODE),
+    d_far, d_near, d_relay, d_total, d_finish, d_drain = reduction(
+        D_PAIRS, lambda a, b: a * b, lambda v: jnp.log(v) * (1.0 / CODE),
         de, dd2, dl1, dr1, dzs, dzr, dacc, drift_code,
         d2send, d2recv, d1send, d1recv, dzsend, dzrecv,
     )
-    o_run, o_finish, o_drain = reduction(
-        lambda a, b: a + b, lambda v: v,
+    o_far, o_near, o_relay, o_total, o_finish, o_drain = reduction(
+        O_PAIRS, lambda a, b: a + b, lambda v: v,
         oe, od2, ol1, or1, ozs, ozr, oacc, lambda k, q: oe[k, q].astype(F32),
         o2send, o2recv, o1send, o1recv, ozsend, ozrecv,
     )
@@ -228,6 +217,16 @@
             de[k, x_far] = drift_code(k, x_far).astype(BF16)
             de[k, near_side] = drift_code(k, near_side).astype(BF16)
 
+    for j in range(first_sends):
+        y_block(j)
+    d_encode(D_PAIRS[0])
+    d_far(D_PAIRS[0])
+    d_near(D_PAIRS[0])
+    d_encode(D_PAIRS[1])
+    d_far(D_PAIRS[1])
+    for j in range(first_sends, NF):
+        y_block(j)
+
     def y_arrival(source):
         return pltpu.make_async_remote_copy(
             src_ref=xs.at[0], dst_ref=xr.at[source], send_sem=ysend.at[0], recv_sem=yrecv.at[source],
@@ -240,7 +239,7 @@
         return jnp.dot(a, b, preferred_element_type=F32)
 
     def newton():
-        for step, dy in enumerate((0, 1, 3, 2)):
+        for step, dy in enumerate((0, 2, 1, 3)):
             first = ((y + dy) % NY) * 2
             if dy:
                 y_arrival(first).wait_recv()
@@ -269,40 +268,70 @@
         ).astype(BF16)
         scale[...] = jnp.broadcast_to(inverse, scale.shape)
 
-    def between(s):
-        if s == 2:
-            for j in range(NY):
-                if SENDS[j][0]:
-                    y_copy(j).wait_send()
-            for j in range(NY, NF):
-                if SENDS[j][0]:
-                    y_copy(j).start()
-
+    def fold_copy(n):
+        k = FOLDED[n]
+        return pltpu.make_async_remote_copy(
+            src_ref=oe.at[k], dst_ref=fold.at[n], send_sem=fold_sem.at[n], recv_sem=fold_sem.at[2 + n],
+            device_id=(((z + k) % NZ) * NX + x, f), device_id_type=MESH,
+        )
+
+    def orth(k):
+        block = xr[(z + k) % NZ]
+        out = (COEF_A * COEF_A) * block.astype(F32) + dot(block, both[...])
+        out = (out * scale[0:1, 0:1]).astype(BF16)
+        for q in range(NX):
+            oe[k, q] = out[:, q * LANES:(q + 1) * LANES]
+
+    def o_open():
+        newton()
+        for k in O_PAIRS[0]:
+            orth(k)
+            o_far((k,))
+            o_near((k,))
+        for n in range(len(FOLDED)):
+            orth(FOLDED[n])
+            fold_copy(n).start()
+        for k in (5, 2, 6):
+            orth(k)
+            o_far((k,))
+        orth(0)
+
+    last = len(D_PAIRS) - 1
+    for s in range(last + 1):
+        if s + 2 <= last:
+            d_encode(D_PAIRS[s + 2])
+        d_relay(D_PAIRS[s])
+        if s + 1 <= last:
+            d_near(D_PAIRS[s + 1])
+        if s + 2 <= last:
+            d_far(D_PAIRS[s + 2])
+        if s:
+            d_total(D_PAIRS[s - 1])
+        if s == EARLY:
             @pl.when(core == 0)
             def _():
-                newton()
-
-    d_run(d_encode, between)
+                o_open()
+
+    d_total(D_PAIRS[last])
 
     @pl.when(core == 1)
     def _():
         d_finish()
-        newton()
-
-    def orth(group):
-        for k in group:
-            block = xr[(z + k) % NZ]
-            out = (COEF_A * COEF_A) * block.astype(F32) + dot(block, both[...])
-            out = (out * scale[0:1, 0:1]).astype(BF16)
-            for q in range(NX):
-                oe[k, q] = out[:, q * LANES:(q + 1) * LANES]
-
-    o_run(orth, lambda s: None)
-
-    @pl.when(core == 0)
-    def _():
-        d_finish()
-
+        o_open()
+
+    o_relay((4, 3))
+    o_near((5, 2, 6))
+    o_relay((5, 2, 6))
+    o_total((4, 3))
+    fold_copy(0).wait_recv()
+    fold_copy(1).wait_recv()
+    for q in range(NX):
+        oe[0, q] = (oe[0, q].astype(F32) + fold[0, q].astype(F32) + fold[1, q].astype(F32)).astype(BF16)
+    o_far((0,))
+    o_near((0,))
+    o_total((5, 2, 6))
+    o_relay((0,))
+    o_total((0,))
     o_finish()
 
     swap_copy = pltpu.make_async_remote_copy(
@@ -314,6 +343,13 @@
     @pl.when(z != f)
     def _():
         swap_copy.start()
+
+    @pl.when(core == 0)
+    def _():
+        d_finish()
+
+    @pl.when(z != f)
+    def _():
         swap_copy.wait_recv()
         oacc[...] = trecv[...].astype(F32)
 
@@ -321,12 +357,14 @@
 
     for j in range(NF):
         dy, c = SENDS[j]
-        if dy and j >= NY:
+        if dy:
             y_copy(j).wait_send()
         if not dy:
             @pl.when(core != c)
             def _():
                 y_copy(j).wait_send()
+    fold_copy(0).wait_send()
+    fold_copy(1).wait_send()
     d_drain()
     o_drain()
 
@@ -341,17 +379,12 @@
     hbm = pl.BlockSpec(memory_space=pl.ANY)
     out = jax.ShapeDtypeStruct((rows, LANES), F32)
 
-    def reduce_buffers():
-        piece = (rows, LANES)
-        return [
-            pltpu.VMEM((NZ, NX) + piece, BF16),
-            pltpu.VMEM((NZ,) + piece, BF16),
-            pltpu.VMEM((NZ,) + piece, BF16),
-            pltpu.VMEM((NZ,) + piece, BF16),
-            pltpu.VMEM((NZ,) + piece, BF16),
-            pltpu.VMEM((NZ,) + piece, BF16),
-            pltpu.VMEM(piece, F32),
-        ]
+    piece = (rows, LANES)
+    reduce_buffers = [
+        pltpu.VMEM((NZ, NX) + piece, BF16),
+        *[pltpu.VMEM((NZ,) + piece, BF16)] * 5,
+        pltpu.VMEM(piece, F32),
+    ]
 
     def sems(n):
         return pltpu.SemaphoreType.DMA((n,))
@@ -371,15 +404,17 @@
             pltpu.VMEM((BLK, BLK), F32),
             pltpu.VMEM((BLK, BLK), BF16),
             pltpu.VMEM((8, LANES), F32),
-            *reduce_buffers(),
-            *reduce_buffers(),
-            pltpu.VMEM((rows, LANES), BF16),
-            pltpu.VMEM((rows, LANES), BF16),
+            *reduce_buffers,
+            *reduce_buffers,
+            pltpu.VMEM((len(FOLDED), NX) + piece, BF16),
+            pltpu.VMEM(piece, BF16),
+            pltpu.VMEM(piece, BF16),
             sems(3 * NF),
             sems(NF),
             sems(NF),
             *reduce_sems,
             *reduce_sems,
+            sems(2 * len(FOLDED)),
             sems(2),
         ],
         compiler_params=pltpu.CompilerParams(

time: 73.3 us -> 71.1 us (0.970)
  Pallas kernels: 70.9 us -> 68.7 us
    pallas_call x1, Pallas kernels: 70.9 us -> 68.7 us  [on_device(): total = call(gradient, momentum, drift)]
where the time goes in v3:
time: 71.1 us; the launch traced here: 71 us
  Pallas kernels  68.7 us (97%)
  other arithmetic  1.68 us (2%)
    pallas_call x1, Pallas kernels, on_device(): total = call(gradient, momentum, drift)  68.7 us
    sub x1, other arithmetic, on_device(): outer_weights - OUTER_LR * (pseudo + OUTER_BETA * new_momentum)  1.68 us

profile of v3, /device:TPU:1, one launch (start us, length us, event | category | flops | bytes accessed | tf_op | source)
XLA Modules:
  0.0 71.0 jit_solution(14449215823822115907)
XLA Ops:
  0.6 0.0 copy-start.1
  0.6 0.0 copy-start
  0.7 68.7 %outer_step.1 = f32[320,128]{1,0:T(8,128)} custom-call(bf16[1,320,4096]{2,1,0:T(8,128)(2,1)} %g_hbm.1, bf16[1,320,4096]{2,1,0:T(8,128)(2,1)} %m_hbm.1, f32[1,320,4096]{2,1,0:T(8,128)} %d_hbm.1), custom_call_target="tpu_custom_call" | custom-call | tf_op jit(solution)/shard_map/outer_step/pallas_call | solution.py:425
  69.3 0.0 copy-done.1
  69.3 0.0 copy-done
  69.4 1.7 %multiply_subtract_fusion = (f32[320,128]{1,0:T(8,128)}, f32[320,128]{1,0:T(8,128)}) fusion(f32[320,128]{1,0:T(8,128)S(1)} %copy-done, f32[320,128]{1,0:T(8,128)} %outer_step.1, f32[320,128]{1,0:T(8,128)S(1)} %copy-done.1), kind=kLoop, calls=%fused_computation | loop fusion | flops 286720 | bytes 819200 | tf_op jit(solution)/shard_map/sub | solution.py:428
Async XLA Ops:
  0.6 68.7 %copy-start.1 = (f32[320,128]{1,0:T(8,128)S(1)}, f32[320,128]{1,0:T(8,128)}, u32[]{:S(2)}) copy-start(f32[320,128]{1,0:T(8,128)} %param.9) | copy-start | bytes 491524
  0.6 68.7 %copy-start = (f32[320,128]{1,0:T(8,128)S(1)}, f32[320,128]{1,0:T(8,128)}, u32[]{:S(2)}) copy-start(f32[320,128]{1,0:T(8,128)} %param.8) | copy-start | bytes 491524

commit v4 on v3

--- a/solution.py
+++ b/solution.py
@@ -41,7 +41,7 @@
     oe, od2, ol1, or1, ozs, ozr, oacc, fold, tsend, trecv,
     load_sem, ysend, yrecv,
     d2send, d2recv, d1send, d1recv, dzsend, dzrecv,
-    o2send, o2recv, o1send, o1recv, ozsend, ozrecv, fold_sem, tsem,
+    o2send, o2recv, o1send, o1recv, ozsend, ozrecv, fold_send, fold_recv, tsem,
 ):
     isl = lax.axis_index("island")
     f = lax.axis_index("fsdp")
@@ -268,12 +268,21 @@
         ).astype(BF16)
         scale[...] = jnp.broadcast_to(inverse, scale.shape)
 
-    def fold_copy(n):
-        k = FOLDED[n]
+    fold_order = (x_far, x_right, x_left, x)
+
+    def fold_copy(n, i):
+        k, q = FOLDED[n], fold_order[i]
         return pltpu.make_async_remote_copy(
-            src_ref=oe.at[k], dst_ref=fold.at[n], send_sem=fold_sem.at[n], recv_sem=fold_sem.at[2 + n],
+            src_ref=oe.at[k, q], dst_ref=fold.at[n, q],
+            send_sem=fold_send.at[NX * n + i], recv_sem=fold_recv.at[NX * n + i],
             device_id=(((z + k) % NZ) * NX + x, f), device_id_type=MESH,
         )
+
+    def fold_in(i):
+        q = fold_order[i]
+        fold_copy(0, i).wait_recv()
+        fold_copy(1, i).wait_recv()
+        oe[0, q] = (oe[0, q].astype(F32) + fold[0, q].astype(F32) + fold[1, q].astype(F32)).astype(BF16)
 
     def orth(k):
         block = xr[(z + k) % NZ]
@@ -284,13 +293,14 @@
 
     def o_open():
         newton()
+        for n in range(len(FOLDED)):
+            orth(FOLDED[n])
+            for i in range(NX):
+                fold_copy(n, i).start()
         for k in O_PAIRS[0]:
             orth(k)
             o_far((k,))
             o_near((k,))
-        for n in range(len(FOLDED)):
-            orth(FOLDED[n])
-            fold_copy(n).start()
         for k in (5, 2, 6):
             orth(k)
             o_far((k,))
@@ -320,17 +330,18 @@
         o_open()
 
     o_relay((4, 3))
-    o_near((5, 2, 6))
+    o_near((5, 2))
+    fold_in(0)
+    o_far((0,))
+    o_near((6,))
     o_relay((5, 2, 6))
     o_total((4, 3))
-    fold_copy(0).wait_recv()
-    fold_copy(1).wait_recv()
-    for q in range(NX):
-        oe[0, q] = (oe[0, q].astype(F32) + fold[0, q].astype(F32) + fold[1, q].astype(F32)).astype(BF16)
-    o_far((0,))
+    fold_in(1)
     o_near((0,))
+    fold_in(2)
+    o_relay((0,))
     o_total((5, 2, 6))
-    o_relay((0,))
+    fold_in(3)
     o_total((0,))
     o_finish()
 
@@ -363,8 +374,9 @@
             @pl.when(core != c)
             def _():
                 y_copy(j).wait_send()
-    fold_copy(0).wait_send()
-    fold_copy(1).wait_send()
+    for n in range(len(FOLDED)):
+        for i in range(NX):
+            fold_copy(n, i).wait_send()
     d_drain()
     o_drain()
 
@@ -414,7 +426,8 @@
             sems(NF),
             *reduce_sems,
             *reduce_sems,
-            sems(2 * len(FOLDED)),
+            sems(len(FOLDED) * NX),
+            sems(len(FOLDED) * NX),
             sems(2),
         ],
         compiler_params=pltpu.CompilerParams(

time: 71.1 us -> 70.4 us (level)
  Pallas kernels: 68.7 us -> 67.8 us
    pallas_call x1, Pallas kernels: 68.7 us -> 67.8 us  [on_device(): total = call(gradient, momentum, drift)]
where the time goes in v4:
time: 70.4 us; the launch traced here: 70.2 us
  Pallas kernels  67.8 us (96%)
  other arithmetic  1.68 us (2%)
    pallas_call x1, Pallas kernels, on_device(): total = call(gradient, momentum, drift)  67.8 us
    sub x1, other arithmetic, on_device(): outer_weights - OUTER_LR * (pseudo + OUTER_BETA * new_momentum)  1.68 us

profile of v4, /device:TPU:1, one launch (start us, length us, event | category | flops | bytes accessed | tf_op | source)
XLA Modules:
  0.0 70.2 jit_solution(9867922786724046864)
XLA Ops:
  0.6 0.0 copy-start.1
  0.6 0.0 copy-start
  0.7 67.8 %outer_step.1 = f32[320,128]{1,0:T(8,128)} custom-call(bf16[1,320,4096]{2,1,0:T(8,128)(2,1)} %g_hbm.1, bf16[1,320,4096]{2,1,0:T(8,128)(2,1)} %m_hbm.1, f32[1,320,4096]{2,1,0:T(8,128)} %d_hbm.1), custom_call_target="tpu_custom_call" | custom-call | tf_op jit(solution)/shard_map/outer_step/pallas_call | solution.py:438
  68.5 0.0 copy-done.1
  68.5 0.0 copy-done
  68.5 1.7 %multiply_subtract_fusion = (f32[320,128]{1,0:T(8,128)}, f32[320,128]{1,0:T(8,128)}) fusion(f32[320,128]{1,0:T(8,128)S(1)} %copy-done, f32[320,128]{1,0:T(8,128)} %outer_step.1, f32[320,128]{1,0:T(8,128)S(1)} %copy-done.1), kind=kLoop, calls=%fused_computation | loop fusion | flops 286720 | bytes 819200 | tf_op jit(solution)/shard_map/sub | solution.py:441
Async XLA Ops:
  0.6 67.8 %copy-start.1 = (f32[320,128]{1,0:T(8,128)S(1)}, f32[320,128]{1,0:T(8,128)}, u32[]{:S(2)}) copy-start(f32[320,128]{1,0:T(8,128)} %param.9) | copy-start | bytes 491524
  0.6 67.8 %copy-start = (f32[320,128]{1,0:T(8,128)S(1)}, f32[320,128]{1,0:T(8,128)}, u32[]{:S(2)}) copy-start(f32[320,128]{1,0:T(8,128)} %param.8) | copy-start | bytes 491524

commit v5 on v4

--- a/solution.py
+++ b/solution.py
@@ -177,12 +177,16 @@
                 else:
                     acc[...] = finish_with(part)
 
+        def gather(ks):
+            for k in ks:
+                zcopy(k).wait_recv()
+            part = finish_with(zr[ks[0]].astype(F32))
+            for k in ks[1:]:
+                part = part + finish_with(zr[k].astype(F32))
+            return part
+
         def finish():
-            part = acc[...]
-            for k in over_z:
-                zcopy(k).wait_recv()
-                part = part + finish_with(zr[k].astype(F32))
-            acc[...] = part
+            acc[...] = acc[...] + gather(over_z)
 
         def drain():
             for a, b in groups:
@@ -194,17 +198,17 @@
             for k in over_z:
                 zcopy(k).wait_send()
 
-        return start_far, start_near, relay, total, finish, drain
+        return start_far, start_near, relay, total, finish, gather, drain
 
     def drift_code(k, q):
         return jnp.exp(CODE * dbuf[k, :, pl.ds(pl.multiple_of(q * LANES, LANES), LANES)])
 
-    d_far, d_near, d_relay, d_total, d_finish, d_drain = reduction(
+    d_far, d_near, d_relay, d_total, d_finish, _, d_drain = reduction(
         D_PAIRS, lambda a, b: a * b, lambda v: jnp.log(v) * (1.0 / CODE),
         de, dd2, dl1, dr1, dzs, dzr, dacc, drift_code,
         d2send, d2recv, d1send, d1recv, dzsend, dzrecv,
     )
-    o_far, o_near, o_relay, o_total, o_finish, o_drain = reduction(
+    o_far, o_near, o_relay, o_total, _, o_gather, o_drain = reduction(
         O_PAIRS, lambda a, b: a + b, lambda v: v,
         oe, od2, ol1, or1, ozs, ozr, oacc, lambda k, q: oe[k, q].astype(F32),
         o2send, o2recv, o1send, o1recv, ozsend, ozrecv,
@@ -342,8 +346,9 @@
     o_relay((0,))
     o_total((5, 2, 6))
     fold_in(3)
+    early = o_gather((4, 3))
     o_total((0,))
-    o_finish()
+    oacc[...] = oacc[...] + early + o_gather((5, 2, 6))
 
     swap_copy = pltpu.make_async_remote_copy(
         src_ref=tsend, dst_ref=trecv, send_sem=tsem.at[0], recv_sem=tsem.at[1],

time: 70.4 us -> 70.4 us (level)
  no operation moved by 1% of the time
where the time goes in v5:
time: 70.4 us; the launch traced here: 70.2 us
  Pallas kernels  67.8 us (96%)
  other arithmetic  1.68 us (2%)
    pallas_call x1, Pallas kernels, on_device(): total = call(gradient, momentum, drift)  67.8 us
    sub x1, other arithmetic, on_device(): outer_weights - OUTER_LR * (pseudo + OUTER_BETA * new_momentum)  1.68 us

profile of v5, /device:TPU:1, one launch (start us, length us, event | category | flops | bytes accessed | tf_op | source)
XLA Modules:
  0.0 70.2 jit_solution(294778010318182450)
XLA Ops:
  0.6 0.0 copy-start.1
  0.6 0.0 copy-start
  0.7 67.8 %outer_step.1 = f32[320,128]{1,0:T(8,128)} custom-call(bf16[1,320,4096]{2,1,0:T(8,128)(2,1)} %g_hbm.1, bf16[1,320,4096]{2,1,0:T(8,128)(2,1)} %m_hbm.1, f32[1,320,4096]{2,1,0:T(8,128)} %d_hbm.1), custom_call_target="tpu_custom_call" | custom-call | tf_op jit(solution)/shard_map/outer_step/pallas_call | solution.py:443
  68.5 0.0 copy-done.1
  68.5 0.0 copy-done
  68.5 1.7 %multiply_subtract_fusion = (f32[320,128]{1,0:T(8,128)}, f32[320,128]{1,0:T(8,128)}) fusion(f32[320,128]{1,0:T(8,128)S(1)} %copy-done, f32[320,128]{1,0:T(8,128)} %outer_step.1, f32[320,128]{1,0:T(8,128)S(1)} %copy-done.1), kind=kLoop, calls=%fused_computation | loop fusion | flops 286720 | bytes 819200 | tf_op jit(solution)/shard_map/sub | solution.py:446
Async XLA Ops:
  0.6 67.8 %copy-start.1 = (f32[320,128]{1,0:T(8,128)S(1)}, f32[320,128]{1,0:T(8,128)}, u32[]{:S(2)}) copy-start(f32[320,128]{1,0:T(8,128)} %param.9) | copy-start | bytes 491524
  0.6 67.8 %copy-start = (f32[320,128]{1,0:T(8,128)S(1)}, f32[320,128]{1,0:T(8,128)}, u32[]{:S(2)}) copy-start(f32[320,128]{1,0:T(8,128)} %param.8) | copy-start | bytes 491524
